TPU v7x, 32 devices: a whole 2x2x4 slice. The times are simulated.
32 devices in a mesh: groups: 2 (over y), row: 4 (over z), col: 4 (over x, core).
Axes of the slice: x: 2, y: 2, z: 4, core: 2. Of those that a mesh axis runs over, the one named last changes fastest.
Arguments:
- hamiltonian: float32 [4096, 2048], P(('groups', 'row'), 'col'), parts along dimension 0, as said below
- pattern: int32 [16, 8], P(('groups', 'row'), 'col'), parts along dimension 0, may hold values from 0 to 1, as said below
- vectors: float32 [4096, 512], P(('groups', 'col')), parts along dimension 0, may hold values from -6 to 6
- damp_lower: float32 [2], P('groups'), parts along dimension 0, may hold values from -0.5 to -0.1
- damp_upper: float32 [2], P('groups'), parts along dimension 0, may hold values from 1 to 1.4
- lowest: float32 [2], P('groups'), parts along dimension 0, may hold values from -1.3 to -0.9
Outputs:
- filtered: float32 [4096, 512], P(('groups', 'row')), parts along dimension 0
There are 2 independent parts, one for each index of `groups`. A program takes and returns all parts, laid end to end along the dimension named above; each array names one. Nothing has to cross between parts.
Inputs may be any that keep to these rules, and one draw needn't show every extreme that they name: Symmetric: hamiltonian[i, j] equals hamiltonian[j, i]. pattern[I, J] equals pattern[J, I], and every diagonal entry is 1.
All inputs are finite; a program needn't handle non-finite values.
Results may differ from a plain program's by a relative error of at most 0.0001.
Values sent between devices are 32-bit elements; how exact they have to be, the bound alone decides.
A program may use at most 64 MiB of HBM per device.

v0:
```python
import jax
import jax.numpy as jnp
from jax import lax
from jax.sharding import PartitionSpec as P

DEGREE = 3


def product(left, right, transposed):
    if transposed:
        contract_dims = (((0,), (0,)), ((), ()))
    else:
        contract_dims = (((1,), (0,)), ((), ()))
    return lax.dot_general(
        left,
        right,
        contract_dims,
        precision=lax.Precision.HIGHEST,
        preferred_element_type=jnp.float32,
    )


def tile_product(masked_tile, current, transposed):
    return product(masked_tile, current, transposed)


def finish_step(partial_term, previous, factor, coefficient, transposed):
    if transposed:
        summed = lax.psum(partial_term, "row")
    else:
        summed = lax.psum(partial_term, "col")
    result = summed * factor
    if previous is not None:
        result = result - coefficient * previous
    return result


def local(hamiltonian, pattern, vectors, damp_lower, damp_upper, lowest):
    block_size = hamiltonian.shape[0] // pattern.shape[0]
    block_mask = jnp.repeat(jnp.repeat(pattern, block_size, axis=0), block_size, axis=1).astype(
        jnp.float32
    )
    masked_tile = hamiltonian * block_mask
    on_diagonal = (lax.axis_index("row") == lax.axis_index("col")).astype(jnp.float32)
    half_width = (damp_upper[0] - damp_lower[0]) * 0.5
    centre = (damp_upper[0] + damp_lower[0]) * 0.5
    ratio_now = half_width / (lowest[0] - centre)
    twice_inverse = 2.0 / ratio_now
    previous = None
    current = vectors
    for degree_step in range(DEGREE):
        transposed = degree_step % 2 == 1
        partial_term = (
            tile_product(masked_tile, current, transposed) - on_diagonal * centre * current
        )
        if degree_step == 0:
            updated = finish_step(partial_term, None, ratio_now / half_width, 0.0, transposed)
        else:
            ratio_next = 1.0 / (twice_inverse - ratio_now)
            updated = finish_step(
                partial_term,
                previous,
                2.0 * ratio_next / half_width,
                ratio_now * ratio_next,
                transposed,
            )
            ratio_now = ratio_next
        previous = current
        current = updated
    return current


def solution(mesh):
    return jax.shard_map(
        local,
        mesh=mesh,
        in_specs=(
            P(("groups", "row"), "col"),
            P(("groups", "row"), "col"),
            P(("groups", "col"), None),
            P("groups"),
            P("groups"),
            P("groups"),
        ),
        out_specs=P(("groups", "row"), None),
        check_vma=False,
    )
```

profile of v0, /device:TPU:0, one launch (start us, length us, event | category | flops | bytes accessed | tf_op | source)
XLA Modules:
  0.0 157.9 jit_solution(18331462456285189686)
XLA Ops:
  6.5 0.0 all-reduce.4.cloned.1.call-start
  7.2 0.0 copy-start.2
  7.9 0.0 copy-done.2
  7.9 0.6 broadcast_in_dim.7
  8.5 0.1 copy.7
  8.6 0.0 copy-start.1
  8.6 1.5 mul.76
  10.1 0.0 copy-done.1
  10.2 2.8 %convolution_subtract_fusion.2 = f32[512,512]{1,0:T(8,128)} fusion(f32[512,512]{1,0:T(8,128)S(1)} %mul.76, f32[512,512]{1,0:T(8,128)S(1)} %copy-done.1, f32[]{:T(128)S(6)} %mul.79), kind=kOutput, calls=%fused_computation.2 | convolution fusion | flops 1611137024 | bytes 3145732 | tf_op jit(solution)/shard_map/dot_general | solution.py:14
  13.0 0.0 all-reduce.4.cloned.1.call-update
  13.0 0.0 all-reduce.6.cloned.1.call-start
  13.7 38.2 %all-reduce.4.cloned.1.call-done = f32[512,512]{1,0:T(8,128)} async-done(((f32[512,512]{1,0:T(8,128)}), f32[512,512]{1,0:T(8,128)}) %all-reduce.4.cloned.1.call-update) | async-done | bytes 1048592 | tf_op jit(solution)/shard_map/psum | solution.py:31
  52.0 4.4 %convolution_subtract_fusion.1 = f32[512,512]{1,0:T(8,128)} fusion(f32[512,512]{1,0:T(8,128)S(1)} %mul.76, f32[512,512]{1,0:T(8,128)} %all-reduce.4.cloned.1.call-done, f32[]{:T(128)S(6)} %div.21, f32[]{:T(128)S(6)} %mul.79), kind=kOutput, calls=%fused_computation.1 | convolution fusion | flops 1611661312 | bytes 3145736 | tf_op jit(solution)/shard_map/dot_general | solution.py:14
  56.4 0.0 all-reduce.6.cloned.1.call-update
  56.4 0.0 all-reduce.8.cloned.1.call-start
  56.6 52.1 %all-reduce.6.cloned.1.call-done = f32[512,512]{1,0:T(8,128)} async-done(((f32[512,512]{1,0:T(8,128)}), f32[512,512]{1,0:T(8,128)}) %all-reduce.6.cloned.1.call-update) | async-done | bytes 1048592 | tf_op jit(solution)/shard_map/psum | solution.py:29
  108.7 4.6 %convolution_subtract_fusion = f32[512,512]{1,0:T(8,128)} fusion(f32[512,512]{1,0:T(8,128)S(1)} %mul.76, f32[512,512]{1,0:T(8,128)S(1)} %copy-done.1, f32[512,512]{1,0:T(8,128)} %all-reduce.6.cloned.1.call-done, f32[]{:T(128)S(6)} %mul.90, f32[]{:T(128)S(6)} %div.25, f32[]{:T(128)S(6)} %mul.79), kind=kOutput, calls=%fused_computation | convolution fusion | flops 1612709888 | bytes 4194316 | tf_op jit(solution)/shard_map/dot_general | solution.py:14
  113.3 0.0 copy-start
  113.3 0.0 all-reduce.8.cloned.1.call-update
  113.4 35.5 %all-reduce.8.cloned.1.call-done = f32[512,512]{1,0:T(8,128)} async-done(((f32[512,512]{1,0:T(8,128)}), f32[512,512]{1,0:T(8,128)}) %all-reduce.8.cloned.1.call-update) | async-done | bytes 1048592 | tf_op jit(solution)/shard_map/psum | solution.py:31
  149.0 0.0 copy-done
  149.0 2.4 %multiply_subtract_fusion = f32[512,512]{1,0:T(8,128)} fusion(f32[512,512]{1,0:T(8,128)} %all-reduce.8.cloned.1.call-done, f32[512,512]{1,0:T(8,128)S(1)} %copy-done, f32[]{:T(128)S(6)} %mul.97, f32[]{:T(128)S(6)} %div.27, f32[]{:T(128)S(6)} %div.21), kind=kLoop, calls=%fused_computation.3 | loop fusion | flops 1048576 | bytes 3145740 | tf_op jit(solution)/shard_map/sub | solution.py:34
  (2 shorter events, 0.0 us)
Async XLA Ops:
  6.5 45.4 %all-reduce.4.cloned.1.call-start = ((), (), s32[]{:S(2)}) async-start(), calls=%async_computation | async-start | bytes 2097152 | tf_op jit(solution)/shard_map/psum | solution.py:31
  7.2 0.7 copy-start.2
  8.6 1.5 copy-start.1
  13.0 95.7 %all-reduce.6.cloned.1.call-start = ((), (), s32[]{:S(2)}) async-start(), calls=%async_computation.1 | async-start | bytes 2097152 | tf_op jit(solution)/shard_map/psum | solution.py:29
  56.4 92.6 %all-reduce.8.cloned.1.call-start = ((), (), s32[]{:S(2)}) async-start(), calls=%async_computation.2 | async-start | bytes 2097152 | tf_op jit(solution)/shard_map/psum | solution.py:31
  113.3 35.6 %copy-start = (f32[512,512]{1,0:T(8,128)S(1)}, f32[512,512]{1,0:T(8,128)}, u32[]{:S(2)}) copy-start(f32[512,512]{1,0:T(8,128)} %all-reduce.4.cloned.1.call-done) | copy-start | bytes 3145732
Sparse Core Ops, SparseCore 0:
  13.1 38.8 all-reduce.3
  56.5 52.1 all-reduce.5
  113.5 35.4 all-reduce.7
where the time goes:
time: 158 us
  waiting for transfers between devices  126 us (80%)
  between operations  15.4 us (10%)
  matrix products  11.8 us (7%)
  other arithmetic  3.96 us (3%)
    psum x2, waiting for transfers between devices, finish_step(): summed = lax.psum(partial_term, 'col')  73.7 us
    psum x1, waiting for transfers between devices, finish_step(): summed = lax.psum(partial_term, 'row')  52.1 us
    dot_general x3, matrix products, product(): lax.dot_general(left, right, contract_dims, precision=lax.Precision.HIGHE...  11.8 us
  transfers between devices with their start and end apart: 3, of which 3 were waited for; matrix products, arithmetic and copies ran while one was open for 0% of the time, Pallas kernels for 0%

commit v1 on v0

v1 whole, which is shorter than its diff:
```python
import functools

import jax
import jax.numpy as jnp
from jax import lax
from jax.experimental import pallas as pl
from jax.experimental.pallas import tpu as pltpu
from jax.sharding import PartitionSpec as P

MESH = pl.DeviceIdType.MESH
CHUNKS = 2
PIECES = 8
LAG = 2


def split(value):
    high = value.astype(jnp.bfloat16)
    low = (value - high.astype(jnp.float32)).astype(jnp.bfloat16)
    return high, low


def dot3(high, low, right):
    right_high, right_low = split(right)
    dot = functools.partial(jnp.dot, preferred_element_type=jnp.float32)
    return dot(high, right_high) + (dot(high, right_low) + dot(low, right_high))


class Line:
    def __init__(self, axis, length, place, stride, index, count, lag, bufs, sems):
        self.axis, self.length, self.place = axis, length, place
        self.up, self.down = index + stride, index - stride
        self.count, self.lag = count, lag
        self.own, self.from_down, self.from_up, self.to_up, self.to_down, self.total = bufs
        self.sems = sems

    def clear(self):
        @pl.when(self.place == 0)
        def _():
            self.from_down[...] = jnp.zeros_like(self.from_down)

        @pl.when(self.place == self.length - 1)
        def _():
            self.from_up[...] = jnp.zeros_like(self.from_up)

    def copy_up(self, s):
        return pltpu.make_async_remote_copy(
            self.to_up.at[s], self.from_down.at[s], self.sems.at[0, s], self.sems.at[1, s],
            device_id={self.axis: self.up}, device_id_type=MESH)

    def copy_down(self, s):
        return pltpu.make_async_remote_copy(
            self.to_down.at[s], self.from_up.at[s], self.sems.at[2, s], self.sems.at[3, s],
            device_id={self.axis: self.down}, device_id_type=MESH)

    def step(self, t, first, end):
        last = self.length - 1
        behind = last - self.place
        s = t - self.lag * self.place

        @pl.when((s >= first) & (s < end))
        def _():
            @pl.when(self.place > 0)
            def _():
                self.copy_up(s).wait_recv()

            @pl.when(self.place < last)
            def _():
                self.to_up[s] = self.own[s] + self.from_down[s]
                self.copy_up(s).start()

        r = t - self.lag * behind

        @pl.when((r >= first) & (r < end))
        def _():
            @pl.when(self.place < last)
            def _():
                self.copy_down(r).wait_recv()

            @pl.when(self.place > 0)
            def _():
                self.to_down[r] = self.own[r] + self.from_up[r]
                self.copy_down(r).start()

        u = t - self.lag * jnp.maximum(self.place, behind)

        @pl.when((u >= first) & (u < end))
        def _():
            self.total[u] = (self.from_down[u] + self.own[u]) + self.from_up[u]

    def steps(self, start, stop, first, end):
        def body(t, carry):
            self.step(t, first, end)
            return carry

        lax.fori_loop(start, stop, body, 0)

    def drain(self):
        def body(s, carry):
            @pl.when(self.place < self.length - 1)
            def _():
                self.copy_up(s).wait_send()

            @pl.when(self.place > 0)
            def _():
                self.copy_down(s).wait_send()
            return carry

        lax.fori_loop(0, self.count, body, 0)


def kernel(rows, cols, pattern, lower, upper, lowest, h_ref, v_ref, out_ref,
           h_own, h_pair, high, low, high_t, low_t, v_pair, part_out, part_in,
           x1_bufs, z_bufs, x3_bufs, x1_sems, z_sems, x3_sems, pair_sems, out_sems):
    row, col = lax.axis_index("row"), lax.axis_index("col")
    core = lax.rem(col, 2)
    x, chips = col // 2, cols // 2
    pair = {"col": col + 1 - 2 * core}
    size = h_ref.shape[0]
    half = v_ref.shape[1] // 2
    wide = half // CHUNKS

    barrier = pltpu.get_barrier_semaphore()
    pl.semaphore_signal(barrier, inc=1, device_id=pair, device_id_type=MESH)
    for there, where in ((x > 0, {"col": col - 2}), (x < chips - 1, {"col": col + 2}),
                         (row > 0, {"row": row - 1}), (row < rows - 1, {"row": row + 1})):
        @pl.when(there)
        def _():
            pl.semaphore_signal(barrier, inc=1, device_id=where, device_id_type=MESH)

    half_width = (upper[0] - lower[0]) * 0.5
    centre = (upper[0] + lower[0]) * 0.5
    ratio0 = half_width / (lowest[0] - centre)
    twice_inverse = 2.0 / ratio0
    factor1 = ratio0 / half_width
    ratio1 = 1.0 / (twice_inverse - ratio0)
    factor2 = 2.0 * ratio1 / half_width
    back2 = ratio0 * ratio1
    ratio2 = 1.0 / (twice_inverse - ratio1)
    factor3 = 2.0 * ratio2 / half_width
    back3 = ratio1 * ratio2

    on_diagonal = jnp.where(row == col, centre, 0.0)
    block = size // pattern.shape[0]
    eye = (lax.broadcasted_iota(jnp.int32, (block, block), 0)
           == lax.broadcasted_iota(jnp.int32, (block, block), 1))
    for i in range(pattern.shape[0]):
        for j in range(pattern.shape[1]):
            at = (slice(i * block, (i + 1) * block), slice(j * block, (j + 1) * block))
            value = h_ref[at] * pattern[i, j].astype(jnp.float32)
            if i == j:
                value = value - jnp.where(eye, on_diagonal, 0.0)
            h_own[at] = value
            high[(0,) + at], low[(0,) + at] = split(value)

    xs1 = Line("col", chips, x, 2, col, CHUNKS, 1, x1_bufs, x1_sems)
    zs = Line("row", rows, row, 1, row, CHUNKS * PIECES, LAG, z_bufs, z_sems)
    xs3 = Line("col", chips, x, 2, col, CHUNKS, 1, x3_bufs, x3_sems)

    def mine(j):
        return pl.ds(pl.multiple_of(core * half + j * wide, wide), wide)

    def theirs(j):
        return pl.ds(pl.multiple_of((1 - core) * half + j * wide, wide), wide)

    def part_copy(j):
        return pltpu.make_async_remote_copy(
            part_out.at[j], part_in.at[j], pair_sems.at[0, j], pair_sems.at[1, j],
            device_id=pair, device_id_type=MESH)

    h_copy = pltpu.make_async_remote_copy(
        h_own, h_pair, pair_sems.at[0, CHUNKS], pair_sems.at[1, CHUNKS],
        device_id=pair, device_id_type=MESH)
    v_copy = pltpu.make_async_remote_copy(
        v_ref.at[:, pl.ds(pl.multiple_of((1 - core) * half, half), half)], v_pair,
        pair_sems.at[0, CHUNKS + 1], pair_sems.at[1, CHUNKS + 1],
        device_id=pair, device_id_type=MESH)

    pl.semaphore_wait(barrier, 1 + (x > 0).astype(jnp.int32) + (x < chips - 1).astype(jnp.int32)
                      + (row > 0).astype(jnp.int32) + (row < rows - 1).astype(jnp.int32))

    for j in range(CHUNKS):
        right = jnp.concatenate([v_ref[:, theirs(j)], v_ref[:, mine(j)]], axis=1)
        part = dot3(high[0], low[0], right) * factor1
        part_out[j] = part[:, :wide]
        part_copy(j).start()
        xs1.own[j] = part[:, wide:]
    h_copy.start()
    v_copy.start()
    for line in (xs1, zs, xs3):
        line.clear()
    for j in range(CHUNKS):
        part_copy(j).wait_recv()
        xs1.own[j] = xs1.own[j] + part_in[j]
        begin(xs1, j)
    high_t[0], low_t[0] = split(h_own[...].T)
    h_copy.wait_recv()
    high_t[1], low_t[1] = split(h_pair[...].T)
    high[1], low[1] = split(h_pair[...])
    v_copy.wait_recv()

    keep = jnp.where(row == 0, back2, 0.0)
    keep3 = jnp.where(x == 0, back3, 0.0)
    pieces = (PIECES // 2, 2 * size // PIECES, wide)

    def second(j):
        finish(xs1, j)
        y1 = xs1.total[j]
        for c in range(2):
            before = v_ref[:, mine(j)] if c == 0 else v_pair[:, j * wide:(j + 1) * wide]
            part = dot3(high_t[c], low_t[c], y1) * factor2 - keep * before
            start = j * PIECES + c * (PIECES // 2)
            zs.own[start:start + PIECES // 2] = part.reshape(pieces)

    def third(j):
        part = -keep3 * xs1.total[j]
        for c in range(2):
            start = j * PIECES + c * (PIECES // 2)
            y2 = zs.total[start:start + PIECES // 2].reshape(size, wide)
            part = part + dot3(high[c], low[c], y2) * factor3
        xs3.own[j] = part
        begin(xs3, j)

    def out_copy(j):
        return pltpu.make_async_remote_copy(
            out_ref.at[:, mine(j)], out_ref.at[:, mine(j)], out_sems.at[0, j], out_sems.at[1, j],
            device_id=pair, device_id_type=MESH)

    def out_landed(j):
        return pltpu.make_async_remote_copy(
            out_ref.at[:, theirs(j)], out_ref.at[:, theirs(j)], out_sems.at[0, j],
            out_sems.at[1, j], device_id=pair, device_id_type=MESH)

    tail = LAG * (rows - 1)
    count = CHUNKS * PIECES
    for j in range(CHUNKS):
        second(j)
        zs.steps(j * PIECES, (j + 1) * PIECES, 0, count)
    at = count
    for j in range(CHUNKS):
        until = max(at, (j + 1) * PIECES + tail)
        zs.steps(at, until, 0, count)
        at = until
        third(j)
    for j in range(CHUNKS):
        finish(xs3, j)
        out_ref[:, mine(j)] = xs3.total[j]
        out_copy(j).start()

    for line in (xs1, zs, xs3):
        line.drain()
    for j in range(CHUNKS):
        part_copy(j).wait_send()
        out_copy(j).wait_send()
        out_landed(j).wait_recv()
    h_copy.wait_send()
    v_copy.wait_send()


def begin(line, j):
    line.step(j, j, j + 1)


def finish(line, j):
    for t in range(1, line.length):
        line.step(t + j, j, j + 1)


def local(hamiltonian, pattern, vectors, damp_lower, damp_upper, lowest, rows, cols):
    size = hamiltonian.shape[0]
    count = vectors.shape[1]
    wide = count // 2 // CHUNKS
    f32, bf16 = jnp.float32, jnp.bfloat16

    def line_bufs(*shape):
        return [pltpu.VMEM(shape, f32)] * 6

    def line_sems(n):
        return pltpu.SemaphoreType.DMA((4, n))

    x_shape = (CHUNKS, size, wide)
    z_shape = (CHUNKS * PIECES, 2 * size // PIECES, wide)
    smem = pl.BlockSpec(memory_space=pltpu.SMEM)
    vmem = pl.BlockSpec(memory_space=pltpu.VMEM)
    return pl.pallas_call(
        functools.partial(kernel, rows, cols),
        out_shape=jax.ShapeDtypeStruct((size, count), f32),
        in_specs=[smem] * 4 + [vmem] * 2,
        out_specs=vmem,
        scratch_shapes=[
            pltpu.VMEM((size, size), f32),
            pltpu.VMEM((size, size), f32),
            pltpu.VMEM((2, size, size), bf16),
            pltpu.VMEM((2, size, size), bf16),
            pltpu.VMEM((2, size, size), bf16),
            pltpu.VMEM((2, size, size), bf16),
            pltpu.VMEM((size, count // 2), f32),
            pltpu.VMEM(x_shape, f32),
            pltpu.VMEM(x_shape, f32),
            line_bufs(*x_shape),
            line_bufs(*z_shape),
            line_bufs(*x_shape),
            line_sems(CHUNKS),
            line_sems(CHUNKS * PIECES),
            line_sems(CHUNKS),
            pltpu.SemaphoreType.DMA((2, CHUNKS + 2)),
            pltpu.SemaphoreType.DMA((2, CHUNKS)),
        ],
        compiler_params=pltpu.CompilerParams(
            collective_id=0, has_side_effects=True, vmem_limit_bytes=48 * 2**20),
        cost_estimate=pl.CostEstimate(
            flops=18 * size * size * count, bytes_accessed=12 * size * count, transcendentals=0),
    )(pattern, damp_lower, damp_upper, lowest, hamiltonian, vectors)


def solution(mesh):
    return jax.shard_map(
        functools.partial(local, rows=mesh.shape["row"], cols=mesh.shape["col"]),
        mesh=mesh,
        in_specs=(
            P(("groups", "row"), "col"),
            P(("groups", "row"), "col"),
            P(("groups", "col"), None),
            P("groups"),
            P("groups"),
            P("groups"),
        ),
        out_specs=P(("groups", "row"), None),
        check_vma=False,
    )
```

time: 158 us -> 66.5 us (0.42)
  waiting for transfers between devices: 126 us -> 0 us
  Pallas kernels: 0 us -> 60.9 us
  between operations: 15.4 us -> 1.98 us
  matrix products: 11.8 us -> 0 us
  other arithmetic: 3.96 us -> 0 us
  local copies, waits for them, and re-layouts: 0.72 us -> 3.43 us
    psum x3 -> x0, waiting for transfers between devices: 126 us -> none  [the longest x2 73.7 us: finish_step(): summed = lax.psum(partial_term, 'col')]
    pallas_call x0 -> x1, Pallas kernels: none -> 60.9 us  [local(): pl.pallas_call(functools.partial(kernel, rows, cols), out_shape=jax.Shape...]
    dot_general x3 -> x0, matrix products: 11.8 us -> none  [product(): lax.dot_general(left, right, contract_dims, precision=lax.Precision.HIGHE...]
    unnamed x7, local copies, waits for them, and re-layouts: 0.09 us -> 3.43 us
    sub x1 -> x0, other arithmetic: 2.44 us -> none  [finish_step(): result = result - coefficient * previous]
  transfers between devices with their start and end apart: 3 -> 0, of which waited for: 3 -> 0; matrix products, arithmetic and copies ran while one was open for 0% -> 0% of each run, Pallas kernels for 0% -> 0%
where the time goes in v1:
time: 66.5 us; the launch traced here: 66.3 us
  Pallas kernels  60.9 us (92%)
  local copies, waits for them, and re-layouts  3.43 us (5%)
  between operations  1.98 us (3%)
    pallas_call x1, Pallas kernels, local(): pl.pallas_call(functools.partial(kernel, rows, cols), out_shape=jax.Shape...  60.9 us
    unnamed x7, local copies, waits for them, and re-layouts  3.43 us

profile of v1, /device:TPU:0, one launch (start us, length us, event | category | flops | bytes accessed | tf_op | source)
XLA Modules:
  0.0 66.3 jit_solution(9528640055927169838)
XLA Ops:
  1.3 0.0 copy-start.2
  2.0 0.0 copy-done.2
  2.0 0.0 copy-start
  2.0 1.2 %copy-done = f32[512,512]{1,0:T(8,128)S(1)} copy-done((f32[512,512]{1,0:T(8,128)S(1)}, f32[512,512]{1,0:T(8,128)}, u32[]{:S(2)}) %copy-start) | copy-done | bytes 1048600
  3.2 0.0 copy-start.1
  3.2 1.2 %copy-done.1 = f32[512,512]{1,0:T(8,128)S(1)} copy-done((f32[512,512]{1,0:T(8,128)S(1)}, f32[512,512]{1,0:T(8,128)}, u32[]{:S(2)}) %copy-start.1) | copy-done | bytes 1048600
  4.4 60.9 %shard_map.64 = f32[512,512]{1,0:T(8,128)S(1)} custom-call(s32[2,2]{1,0:T(2,128)S(1)} %copy-done.2, f32[1]{0:T(128)S(6)} %copy.8.lower, f32[1]{0:T(128)S(6)} %copy.9.upper, f32[1]{0:T(128)S(6)} %copy.10.lowest, f32[512,512]{1,0:T(8,128)S(1)} %copy-done, f32[512,512]{1,0:T(8,128)S(1)} %copy-done.1), custom_call_target="tpu_custom_call" | custom-call | flops 2415919104 | bytes 3145728 | tf_op jit(solution)/shard_map/pallas_call | solution.py:284
  65.3 1.0 %copy.11 = f32[512,512]{1,0:T(8,128)} copy(f32[512,512]{1,0:T(8,128)S(1)} %shard_map.64) | data formatting | bytes 2097152
Async XLA Ops:
  1.3 0.7 %copy-start.2 = (s32[2,2]{1,0:T(2,128)S(1)}, s32[2,2]{1,0:T(2,128)}, u32[]{:S(2)}) copy-start(s32[2,2]{1,0:T(2,128)} %pattern.1) | copy-start | bytes 52
  2.0 1.2 %copy-start = (f32[512,512]{1,0:T(8,128)S(1)}, f32[512,512]{1,0:T(8,128)}, u32[]{:S(2)}) copy-start(f32[512,512]{1,0:T(8,128)} %h_ref.1) | copy-start | bytes 3145732
  3.2 1.2 %copy-start.1 = (f32[512,512]{1,0:T(8,128)S(1)}, f32[512,512]{1,0:T(8,128)}, u32[]{:S(2)}) copy-start(f32[512,512]{1,0:T(8,128)} %v_ref.1) | copy-start | bytes 3145732

commit v2 on v1

v2 whole, which is shorter than its diff:
```python
import functools

import jax
import jax.numpy as jnp
from jax import lax
from jax.experimental import pallas as pl
from jax.experimental.pallas import tpu as pltpu
from jax.sharding import PartitionSpec as P

MESH = pl.DeviceIdType.MESH
WIDE = 128
PIECES = 4
LAG = 3


def split(value):
    high = value.astype(jnp.bfloat16)
    low = (value - high.astype(jnp.float32)).astype(jnp.bfloat16)
    return high, low


def dot3(high, low, right):
    right_high, right_low = split(right)
    wide = right.shape[1]
    dot = functools.partial(jnp.dot, preferred_element_type=jnp.float32)
    both = dot(high, jnp.concatenate([right_high, right_low], axis=1))
    return both[:, :wide] + (both[:, wide:] + dot(low, right_high))


class Line:
    def __init__(self, axis, length, place, stride, index, count, lag, bufs, sems):
        self.axis, self.length, self.place = axis, length, place
        self.up, self.down = index + stride, index - stride
        self.count, self.lag = count, lag
        self.own, self.from_down, self.from_up, self.to_up, self.to_down, self.total = bufs
        self.sems = sems

    def clear(self):
        @pl.when(self.place == 0)
        def _():
            self.from_down[...] = jnp.zeros_like(self.from_down)

        @pl.when(self.place == self.length - 1)
        def _():
            self.from_up[...] = jnp.zeros_like(self.from_up)

    def copy_up(self, s):
        return pltpu.make_async_remote_copy(
            self.to_up.at[s], self.from_down.at[s], self.sems.at[0, s], self.sems.at[1, s],
            device_id={self.axis: self.up}, device_id_type=MESH)

    def copy_down(self, s):
        return pltpu.make_async_remote_copy(
            self.to_down.at[s], self.from_up.at[s], self.sems.at[2, s], self.sems.at[3, s],
            device_id={self.axis: self.down}, device_id_type=MESH)

    def step(self, t, first, end):
        last = self.length - 1
        behind = last - self.place
        s = t - self.lag * self.place

        @pl.when((s >= first) & (s < end))
        def _():
            @pl.when(self.place > 0)
            def _():
                self.copy_up(s).wait_recv()

            @pl.when(self.place < last)
            def _():
                self.to_up[s] = self.own[s] + self.from_down[s]
                self.copy_up(s).start()

        r = t - self.lag * behind

        @pl.when((r >= first) & (r < end))
        def _():
            @pl.when(self.place < last)
            def _():
                self.copy_down(r).wait_recv()

            @pl.when(self.place > 0)
            def _():
                self.to_down[r] = self.own[r] + self.from_up[r]
                self.copy_down(r).start()

        u = t - self.lag * jnp.maximum(self.place, behind)

        @pl.when((u >= first) & (u < end))
        def _():
            self.total[u] = (self.from_down[u] + self.own[u]) + self.from_up[u]

    def steps(self, start, stop, first, end):
        def body(t, carry):
            self.step(t, first, end)
            return carry

        lax.fori_loop(start, stop, body, 0)

    def drain(self):
        def body(s, carry):
            @pl.when(self.place < self.length - 1)
            def _():
                self.copy_up(s).wait_send()

            @pl.when(self.place > 0)
            def _():
                self.copy_down(s).wait_send()
            return carry

        lax.fori_loop(0, self.count, body, 0)


def kernel(rows, cols, pattern, lower, upper, lowest, h_hbm, v_hbm, out_hbm,
           h_ref, v_ref, high, low, high_t, low_t, part1, pair1, y1, part3, pair3,
           x1_bufs, z_bufs, x3_bufs, x1_sems, z_sems, x3_sems, pair_sems, load_sems, out_sems):
    row, col = lax.axis_index("row"), lax.axis_index("col")
    core = lax.rem(col, 2)
    x, chips = col // 2, cols // 2
    pair = {"col": col + 1 - 2 * core}
    size = h_ref.shape[0]
    half = size // 2
    chunks = v_ref.shape[0]

    barrier = pltpu.get_barrier_semaphore()
    pl.semaphore_signal(barrier, inc=1, device_id=pair, device_id_type=MESH)
    for there, where in ((x > 0, {"col": col - 2}), (x < chips - 1, {"col": col + 2}),
                         (row > 0, {"row": row - 1}), (row < rows - 1, {"row": row + 1})):
        @pl.when(there)
        def _():
            pl.semaphore_signal(barrier, inc=1, device_id=where, device_id_type=MESH)

    def columns(j):
        return pl.ds(j * WIDE, WIDE)

    loads = [pltpu.make_async_copy(h_hbm, h_ref, load_sems.at[chunks])]
    loads += [pltpu.make_async_copy(v_hbm.at[:, columns(j)], v_ref.at[j], load_sems.at[j])
              for j in range(chunks)]
    for load in loads:
        load.start()

    half_width = (upper[0] - lower[0]) * 0.5
    centre = (upper[0] + lower[0]) * 0.5
    ratio0 = half_width / (lowest[0] - centre)
    twice_inverse = 2.0 / ratio0
    factor1 = ratio0 / half_width
    ratio1 = 1.0 / (twice_inverse - ratio0)
    factor2 = 2.0 * ratio1 / half_width
    back2 = ratio0 * ratio1
    ratio2 = 1.0 / (twice_inverse - ratio1)
    factor3 = 2.0 * ratio2 / half_width
    back3 = ratio1 * ratio2
    keep2 = jnp.where(row == 0, back2, 0.0)
    keep3 = jnp.where(col == 0, back3, 0.0)

    xs1 = Line("col", chips, x, 2, col, chunks, 1, x1_bufs, x1_sems)
    zs = Line("row", rows, row, 1, row, chunks * PIECES, LAG, z_bufs, z_sems)
    xs3 = Line("col", chips, x, 2, col, chunks, 1, x3_bufs, x3_sems)
    for line in (xs1, zs, xs3):
        line.clear()

    on_diagonal = jnp.where(row == col, centre, 0.0)
    block = size // pattern.shape[0]
    eye = (lax.broadcasted_iota(jnp.int32, (block, block), 0)
           == lax.broadcasted_iota(jnp.int32, (block, block), 1))
    loads[0].wait()
    for i in range(pattern.shape[0]):
        for j in range(pattern.shape[1]):
            at = (slice(i * block, (i + 1) * block), slice(j * block, (j + 1) * block))
            value = h_ref[at] * pattern[i, j].astype(jnp.float32)
            if i == j:
                value = value - jnp.where(eye, on_diagonal, 0.0)
            h_ref[at] = value
            high[at], low[at] = split(value)

    mine = pl.ds(pl.multiple_of(core * half, half), half)
    theirs = pl.ds(pl.multiple_of((1 - core) * half, half), half)

    def to_pair(kind, j, source, target):
        return pltpu.make_async_remote_copy(
            source, target, pair_sems.at[0, kind, j], pair_sems.at[1, kind, j],
            device_id=pair, device_id_type=MESH)

    def part1_copy(j):
        return to_pair(0, j, part1.at[j, theirs], pair1.at[j])

    def y1_copy(j):
        return to_pair(1, j, y1.at[j, mine], y1.at[j, mine])

    def y1_landed(j):
        return to_pair(1, j, y1.at[j, theirs], y1.at[j, theirs])

    def part3_copy(j):
        return to_pair(2, j, part3.at[j, theirs], pair3.at[j])

    def out_copy(j):
        return to_pair(3, j, xs3.total.at[j], out_hbm.at[mine, columns(j)])

    def out_landed(j):
        return to_pair(3, j, xs3.total.at[j], out_hbm.at[theirs, columns(j)])

    def out_own(j):
        return pltpu.make_async_copy(
            xs3.total.at[j], out_hbm.at[mine, columns(j)], out_sems.at[j])

    pieces = (PIECES, size // PIECES, WIDE)

    def at_pieces(j):
        return pl.ds(j * PIECES, PIECES)

    def first(j):
        loads[1 + j].wait()
        part1[j] = dot3(high[...], low[...], v_ref[j]) * factor1
        if j == 0:
            pl.semaphore_wait(
                barrier, 1 + (x > 0).astype(jnp.int32) + (x < chips - 1).astype(jnp.int32)
                + (row > 0).astype(jnp.int32) + (row < rows - 1).astype(jnp.int32))
        part1_copy(j).start()

    def first_send(j):
        part1_copy(j).wait_recv()
        xs1.own[j] = part1[j, mine] + pair1[j]
        begin(xs1, j)

    def first_end(j):
        finish(xs1, j)
        y1[j, mine] = xs1.total[j]
        y1_copy(j).start()

    def second(j):
        y1_landed(j).wait_recv()
        part = dot3(high_t[...], low_t[...], y1[j]) * factor2 - keep2 * v_ref[j]
        zs.own[at_pieces(j)] = part.reshape(pieces)

    def third(j):
        y2 = zs.total[at_pieces(j)].reshape(size, WIDE)
        part3[j] = dot3(high[...], low[...], y2) * factor3 - keep3 * y1[j]
        part3_copy(j).start()

    def third_send(j):
        part3_copy(j).wait_recv()
        xs3.own[j] = part3[j, mine] + pair3[j]
        begin(xs3, j)

    def third_end(j):
        finish(xs3, j)
        out_copy(j).start()
        out_own(j).start()

    first(0)
    for j in range(chunks):
        if j + 1 < chunks:
            first(j + 1)
        first_send(j)
    high_t[...], low_t[...] = split(h_ref[...].T)
    first_end(0)

    tail = LAG * (rows - 1)
    count = chunks * PIECES
    events = []
    for j in range(chunks):
        if j > 0:
            events.append((j * PIECES - 2, first_end, j))
        events.append((j * PIECES, second, j))
        whole = (j + 1) * PIECES + tail
        events.append((whole, third, j))
        events.append((whole + 1, third_send, j))
        events.append((whole + 5, third_end, j))
    t = 0
    for when, event, j in sorted(events, key=lambda e: e[0]):
        until = min(when, count + tail)
        if until > t:
            zs.steps(t, until, 0, count)
            t = until
        event(j)

    for line in (xs1, zs, xs3):
        line.drain()
    for j in range(chunks):
        part1_copy(j).wait_send()
        y1_copy(j).wait_send()
        part3_copy(j).wait_send()
        out_copy(j).wait_send()
        out_own(j).wait()
        out_landed(j).wait_recv()


def begin(line, j):
    line.step(j, j, j + 1)


def finish(line, j):
    for t in range(1, line.length):
        line.step(t + j, j, j + 1)


def local(hamiltonian, pattern, vectors, damp_lower, damp_upper, lowest, rows, cols):
    size = hamiltonian.shape[0]
    count = vectors.shape[1]
    chunks = count // WIDE
    f32, bf16 = jnp.float32, jnp.bfloat16

    def line_bufs(*shape):
        return [pltpu.VMEM(shape, f32)] * 6

    def sems(*shape):
        return pltpu.SemaphoreType.DMA(shape)

    whole = pltpu.VMEM((chunks, size, WIDE), f32)
    halves = (chunks, size // 2, WIDE)
    smem = pl.BlockSpec(memory_space=pltpu.SMEM)
    hbm = pl.BlockSpec(memory_space=pl.ANY)
    return pl.pallas_call(
        functools.partial(kernel, rows, cols),
        out_shape=jax.ShapeDtypeStruct((size, count), f32),
        in_specs=[smem] * 4 + [hbm] * 2,
        out_specs=hbm,
        scratch_shapes=[
            pltpu.VMEM((size, size), f32),
            whole,
            pltpu.VMEM((size, size), bf16),
            pltpu.VMEM((size, size), bf16),
            pltpu.VMEM((size, size), bf16),
            pltpu.VMEM((size, size), bf16),
            whole,
            pltpu.VMEM(halves, f32),
            whole,
            whole,
            pltpu.VMEM(halves, f32),
            line_bufs(*halves),
            line_bufs(chunks * PIECES, size // PIECES, WIDE),
            line_bufs(*halves),
            sems(4, chunks),
            sems(4, chunks * PIECES),
            sems(4, chunks),
            sems(2, 4, chunks),
            sems(chunks + 1),
            sems(chunks),
        ],
        compiler_params=pltpu.CompilerParams(
            collective_id=0, has_side_effects=True, vmem_limit_bytes=60 * 2**20),
        cost_estimate=pl.CostEstimate(
            flops=18 * size * size * count, bytes_accessed=12 * size * count, transcendentals=0),
    )(pattern, damp_lower, damp_upper, lowest, hamiltonian, vectors)


def solution(mesh):
    return jax.shard_map(
        functools.partial(local, rows=mesh.shape["row"], cols=mesh.shape["col"]),
        mesh=mesh,
        in_specs=(
            P(("groups", "row"), "col"),
            P(("groups", "row"), "col"),
            P(("groups", "col"), None),
            P("groups"),
            P("groups"),
            P("groups"),
        ),
        out_specs=P(("groups", "row"), None),
        check_vma=False,
    )
```

time: 66.5 us -> 58.7 us (0.88)
  Pallas kernels: 60.9 us -> 54.3 us
  local copies, waits for them, and re-layouts: 3.43 us -> 2.26 us
    pallas_call x1, Pallas kernels: 60.9 us -> 54.3 us  [local(): pl.pallas_call(functools.partial(kernel, rows, cols), out_shape=jax.Shape...]
    unnamed x7 -> x1, local copies, waits for them, and re-layouts: 3.43 us -> 2.26 us
where the time goes in v2:
time: 58.7 us; the launch traced here: 58.5 us
  Pallas kernels  54.3 us (93%)
  local copies, waits for them, and re-layouts  2.26 us (4%)
  between operations  1.95 us (3%)
    pallas_call x1, Pallas kernels, local(): pl.pallas_call(functools.partial(kernel, rows, cols), out_shape=jax.Shape...  54.3 us
    unnamed x1, local copies, waits for them, and re-layouts  2.26 us

profile of v2, /device:TPU:0, one launch (start us, length us, event | category | flops | bytes accessed | tf_op | source)
XLA Modules:
  0.0 58.5 jit_solution(16307559982640035901)
XLA Ops:
  1.9 54.3 %shard_map.64 = f32[512,512]{1,0:T(8,128)} custom-call(s32[2,2]{1,0:T(2,128)} %pattern.1, f32[1]{0:T(128)S(6)} %copy.8.lower, f32[1]{0:T(128)S(6)} %copy.9.upper, f32[1]{0:T(128)S(6)} %copy.10.lowest, f32[512,512]{1,0:T(8,128)} %h_hbm.1, f32[512,512]{1,0:T(8,128)} %v_hbm.1), custom_call_target="tpu_custom_call" | custom-call | flops 2415919104 | bytes 3145728 | tf_op jit(solution)/shard_map/pallas_call | solution.py:312
  56.3 2.3 %copy.11 = f32[512,512]{1,0:T(8,128)} copy(f32[512,512]{1,0:T(8,128)} %shard_map.64) | data formatting | bytes 2097152

commit v3 on v2

--- a/solution.py
+++ b/solution.py
@@ -8,7 +8,7 @@
 from jax.sharding import PartitionSpec as P
 
 MESH = pl.DeviceIdType.MESH
-WIDE = 128
+WIDE = 64
 PIECES = 4
 LAG = 3
 
@@ -20,11 +20,22 @@
 
 
 def dot3(high, low, right):
-    right_high, right_low = split(right)
     wide = right.shape[1]
+    right_high = right.astype(jnp.bfloat16).astype(jnp.float32)
+    rights = jnp.concatenate([right_high, right - right_high], axis=1).astype(jnp.bfloat16)
     dot = functools.partial(jnp.dot, preferred_element_type=jnp.float32)
-    both = dot(high, jnp.concatenate([right_high, right_low], axis=1))
-    return both[:, :wide] + (both[:, wide:] + dot(low, right_high))
+    both = dot(high, rights)
+    return both[:, :wide] + (both[:, wide:] + dot(low, rights[:, :wide]))
+
+
+def pack(value):
+    half = value.shape[0] // 2
+    return jnp.concatenate([value[:half], value[half:]], axis=1)
+
+
+def unpack(value):
+    half = value.shape[1] // 2
+    return jnp.concatenate([value[:, :half], value[:, half:]], axis=0)
 
 
 class Line:
@@ -110,16 +121,18 @@
         lax.fori_loop(0, self.count, body, 0)
 
 
-def kernel(rows, cols, pattern, lower, upper, lowest, h_hbm, v_hbm, out_hbm,
-           h_ref, v_ref, high, low, high_t, low_t, part1, pair1, y1, part3, pair3,
+def kernel(rows, cols, pattern, lower, upper, lowest, h_hbm, v_hbm, out_ref,
+           h_ref, h_pair, v_mine, v_theirs, v_pair, high, low, high_t, low_t, part1, pair1,
            x1_bufs, z_bufs, x3_bufs, x1_sems, z_sems, x3_sems, pair_sems, load_sems, out_sems):
     row, col = lax.axis_index("row"), lax.axis_index("col")
     core = lax.rem(col, 2)
     x, chips = col // 2, cols // 2
     pair = {"col": col + 1 - 2 * core}
     size = h_ref.shape[0]
-    half = size // 2
-    chunks = v_ref.shape[0]
+    half = v_mine.shape[1]
+    chunks = half // WIDE
+    mine = pl.ds(pl.multiple_of(core * half, half), half)
+    theirs = pl.ds(pl.multiple_of((1 - core) * half, half), half)
 
     barrier = pltpu.get_barrier_semaphore()
     pl.semaphore_signal(barrier, inc=1, device_id=pair, device_id_type=MESH)
@@ -130,11 +143,11 @@
             pl.semaphore_signal(barrier, inc=1, device_id=where, device_id_type=MESH)
 
     def columns(j):
-        return pl.ds(j * WIDE, WIDE)
-
-    loads = [pltpu.make_async_copy(h_hbm, h_ref, load_sems.at[chunks])]
-    loads += [pltpu.make_async_copy(v_hbm.at[:, columns(j)], v_ref.at[j], load_sems.at[j])
-              for j in range(chunks)]
+        return slice(j * WIDE, (j + 1) * WIDE)
+
+    loads = [pltpu.make_async_copy(h_hbm, h_ref, load_sems.at[0]),
+             pltpu.make_async_copy(v_hbm.at[:, theirs], v_theirs, load_sems.at[1]),
+             pltpu.make_async_copy(v_hbm.at[:, mine], v_mine, load_sems.at[2])]
     for load in loads:
         load.start()
 
@@ -150,7 +163,7 @@
     factor3 = 2.0 * ratio2 / half_width
     back3 = ratio1 * ratio2
     keep2 = jnp.where(row == 0, back2, 0.0)
-    keep3 = jnp.where(col == 0, back3, 0.0)
+    keep3 = jnp.where(x == 0, back3, 0.0)
 
     xs1 = Line("col", chips, x, 2, col, chunks, 1, x1_bufs, x1_sems)
     zs = Line("row", rows, row, 1, row, chunks * PIECES, LAG, z_bufs, z_sems)
@@ -170,101 +183,101 @@
             if i == j:
                 value = value - jnp.where(eye, on_diagonal, 0.0)
             h_ref[at] = value
-            high[at], low[at] = split(value)
-
-    mine = pl.ds(pl.multiple_of(core * half, half), half)
-    theirs = pl.ds(pl.multiple_of((1 - core) * half, half), half)
-
-    def to_pair(kind, j, source, target):
-        return pltpu.make_async_remote_copy(
-            source, target, pair_sems.at[0, kind, j], pair_sems.at[1, kind, j],
+            high[(0,) + at], low[(0,) + at] = split(value)
+
+    def to_pair(n, source, target):
+        return pltpu.make_async_remote_copy(
+            source, target, pair_sems.at[0, n], pair_sems.at[1, n],
             device_id=pair, device_id_type=MESH)
 
-    def part1_copy(j):
-        return to_pair(0, j, part1.at[j, theirs], pair1.at[j])
-
-    def y1_copy(j):
-        return to_pair(1, j, y1.at[j, mine], y1.at[j, mine])
-
-    def y1_landed(j):
-        return to_pair(1, j, y1.at[j, theirs], y1.at[j, theirs])
-
-    def part3_copy(j):
-        return to_pair(2, j, part3.at[j, theirs], pair3.at[j])
+    def part_copy(j):
+        return to_pair(j, part1.at[j], pair1.at[j])
+
+    h_copy = to_pair(chunks, h_ref, h_pair)
+    v_copy = to_pair(chunks + 1, v_theirs, v_pair)
+
+    def at_out(which, j):
+        start = pl.multiple_of(which * half + j * WIDE, 2 * WIDE)
+        return out_ref.at[:, pl.ds(start, 2 * WIDE)]
 
     def out_copy(j):
-        return to_pair(3, j, xs3.total.at[j], out_hbm.at[mine, columns(j)])
+        return pltpu.make_async_remote_copy(
+            at_out(core, j), at_out(core, j), out_sems.at[0, j // 2], out_sems.at[1, j // 2],
+            device_id=pair, device_id_type=MESH)
 
     def out_landed(j):
-        return to_pair(3, j, xs3.total.at[j], out_hbm.at[theirs, columns(j)])
-
-    def out_own(j):
-        return pltpu.make_async_copy(
-            xs3.total.at[j], out_hbm.at[mine, columns(j)], out_sems.at[j])
-
-    pieces = (PIECES, size // PIECES, WIDE)
-
-    def at_pieces(j):
-        return pl.ds(j * PIECES, PIECES)
+        return pltpu.make_async_remote_copy(
+            at_out(1 - core, j), at_out(1 - core, j), out_sems.at[0, j // 2],
+            out_sems.at[1, j // 2], device_id=pair, device_id_type=MESH)
+
+    quarter = PIECES // 2
+    pieces = (quarter, size // PIECES, 2 * WIDE)
+
+    def at_pieces(j, c):
+        return pl.ds(j * PIECES + c * quarter, quarter)
 
     def first(j):
-        loads[1 + j].wait()
-        part1[j] = dot3(high[...], low[...], v_ref[j]) * factor1
+        right = jnp.concatenate([v_theirs[:, columns(j)], v_mine[:, columns(j)]], axis=1)
+        part = dot3(high[0], low[0], right) * factor1
+        part1[j] = pack(part[:, :WIDE])
         if j == 0:
             pl.semaphore_wait(
                 barrier, 1 + (x > 0).astype(jnp.int32) + (x < chips - 1).astype(jnp.int32)
                 + (row > 0).astype(jnp.int32) + (row < rows - 1).astype(jnp.int32))
-        part1_copy(j).start()
+        part_copy(j).start()
+        xs1.own[j] = pack(part[:, WIDE:])
 
     def first_send(j):
-        part1_copy(j).wait_recv()
-        xs1.own[j] = part1[j, mine] + pair1[j]
+        part_copy(j).wait_recv()
+        xs1.own[j] = xs1.own[j] + pair1[j]
         begin(xs1, j)
 
-    def first_end(j):
+    def second(j):
         finish(xs1, j)
-        y1[j, mine] = xs1.total[j]
-        y1_copy(j).start()
-
-    def second(j):
-        y1_landed(j).wait_recv()
-        part = dot3(high_t[...], low_t[...], y1[j]) * factor2 - keep2 * v_ref[j]
-        zs.own[at_pieces(j)] = part.reshape(pieces)
+        y1 = unpack(xs1.total[j])
+        for c, before in enumerate((v_mine, v_pair)):
+            part = dot3(high_t[c], low_t[c], y1) * factor2 - keep2 * before[:, columns(j)]
+            zs.own[at_pieces(j, c)] = pack(part).reshape(pieces)
 
     def third(j):
-        y2 = zs.total[at_pieces(j)].reshape(size, WIDE)
-        part3[j] = dot3(high[...], low[...], y2) * factor3 - keep3 * y1[j]
-        part3_copy(j).start()
-
-    def third_send(j):
-        part3_copy(j).wait_recv()
-        xs3.own[j] = part3[j, mine] + pair3[j]
+        part = jnp.zeros((size, WIDE), jnp.float32)
+        for c in range(2):
+            y2 = zs.total[at_pieces(j, c)].reshape(size // 2, 2 * WIDE)
+            part = part + dot3(high[c], low[c], unpack(y2))
+        xs3.own[j] = pack(part * factor3) - keep3 * xs1.total[j]
         begin(xs3, j)
 
     def third_end(j):
         finish(xs3, j)
-        out_copy(j).start()
-        out_own(j).start()
-
+        if j % 2 == 1:
+            at_out(core, j - 1)[...] = jnp.concatenate(
+                [unpack(xs3.total[j - 1]), unpack(xs3.total[j])], axis=1)
+            out_copy(j - 1).start()
+
+    loads[1].wait()
+    loads[2].wait()
     first(0)
     for j in range(chunks):
         if j + 1 < chunks:
             first(j + 1)
+        if j == 0:
+            h_copy.start()
+            v_copy.start()
         first_send(j)
-    high_t[...], low_t[...] = split(h_ref[...].T)
-    first_end(0)
+    high_t[0], low_t[0] = split(h_ref[...].T)
+    h_copy.wait_recv()
+    high[1], low[1] = split(h_pair[...])
+    high_t[1], low_t[1] = split(h_pair[...].T)
+    v_copy.wait_recv()
 
     tail = LAG * (rows - 1)
     count = chunks * PIECES
     events = []
     for j in range(chunks):
-        if j > 0:
-            events.append((j * PIECES - 2, first_end, j))
         events.append((j * PIECES, second, j))
         whole = (j + 1) * PIECES + tail
         events.append((whole, third, j))
-        events.append((whole + 1, third_send, j))
-        events.append((whole + 5, third_end, j))
+        events.append((whole + 4, third_end, j))
     t = 0
     for when, event, j in sorted(events, key=lambda e: e[0]):
         until = min(when, count + tail)
@@ -276,11 +289,11 @@
     for line in (xs1, zs, xs3):
         line.drain()
     for j in range(chunks):
-        part1_copy(j).wait_send()
-        y1_copy(j).wait_send()
-        part3_copy(j).wait_send()
+        part_copy(j).wait_send()
+    h_copy.wait_send()
+    v_copy.wait_send()
+    for j in range(0, chunks, 2):
         out_copy(j).wait_send()
-        out_own(j).wait()
         out_landed(j).wait_recv()
 
 
@@ -296,7 +309,7 @@
 def local(hamiltonian, pattern, vectors, damp_lower, damp_upper, lowest, rows, cols):
     size = hamiltonian.shape[0]
     count = vectors.shape[1]
-    chunks = count // WIDE
+    chunks = count // 2 // WIDE
     f32, bf16 = jnp.float32, jnp.bfloat16
 
     def line_bufs(*shape):
@@ -305,36 +318,38 @@
     def sems(*shape):
         return pltpu.SemaphoreType.DMA(shape)
 
-    whole = pltpu.VMEM((chunks, size, WIDE), f32)
-    halves = (chunks, size // 2, WIDE)
+    chunk = (chunks, size // 2, 2 * WIDE)
+    square = pltpu.VMEM((size, size), f32)
+    vectors_half = pltpu.VMEM((size, count // 2), f32)
+    squares = pltpu.VMEM((2, size, size), bf16)
     smem = pl.BlockSpec(memory_space=pltpu.SMEM)
     hbm = pl.BlockSpec(memory_space=pl.ANY)
     return pl.pallas_call(
         functools.partial(kernel, rows, cols),
         out_shape=jax.ShapeDtypeStruct((size, count), f32),
         in_specs=[smem] * 4 + [hbm] * 2,
-        out_specs=hbm,
+        out_specs=pl.BlockSpec(memory_space=pltpu.VMEM),
         scratch_shapes=[
-            pltpu.VMEM((size, size), f32),
-            whole,
-            pltpu.VMEM((size, size), bf16),
-            pltpu.VMEM((size, size), bf16),
-            pltpu.VMEM((size, size), bf16),
-            pltpu.VMEM((size, size), bf16),
-            whole,
-            pltpu.VMEM(halves, f32),
-            whole,
-            whole,
-            pltpu.VMEM(halves, f32),
-            line_bufs(*halves),
-            line_bufs(chunks * PIECES, size // PIECES, WIDE),
-            line_bufs(*halves),
+            square,
+            square,
+            vectors_half,
+            vectors_half,
+            vectors_half,
+            squares,
+            squares,
+            squares,
+            squares,
+            pltpu.VMEM(chunk, f32),
+            pltpu.VMEM(chunk, f32),
+            line_bufs(*chunk),
+            line_bufs(chunks * PIECES, size // PIECES, 2 * WIDE),
+            line_bufs(*chunk),
             sems(4, chunks),
             sems(4, chunks * PIECES),
             sems(4, chunks),
-            sems(2, 4, chunks),
-            sems(chunks + 1),
-            sems(chunks),
+            sems(2, chunks + 2),
+            sems(3),
+            sems(2, chunks // 2),
         ],
         compiler_params=pltpu.CompilerParams(
             collective_id=0, has_side_effects=True, vmem_limit_bytes=60 * 2**20),

time: 58.7 us -> 58.1 us (0.990)
  Pallas kernels: 54.3 us -> 53.7 us
    pallas_call x1, Pallas kernels: 54.3 us -> 53.7 us  [local(): pl.pallas_call(functools.partial(kernel, rows, cols), out_shape=jax.Shape...]
where the time goes in v3:
time: 58.1 us; the launch traced here: 57.9 us
  Pallas kernels  53.7 us (92%)
  local copies, waits for them, and re-layouts  2.26 us (4%)
  between operations  1.95 us (3%)
    pallas_call x1, Pallas kernels, local(): pl.pallas_call(functools.partial(kernel, rows, cols), out_shape=jax.Shape...  53.7 us
    unnamed x1, local copies, waits for them, and re-layouts  2.26 us

profile of v3, /device:TPU:0, one launch (start us, length us, event | category | flops | bytes accessed | tf_op | source)
XLA Modules:
  0.0 57.9 jit_solution(15398475526756354865)
XLA Ops:
  1.9 53.7 %shard_map.64 = f32[512,512]{1,0:T(8,128)} custom-call(s32[2,2]{1,0:T(2,128)} %pattern.1, f32[1]{0:T(128)S(6)} %copy.8.lower, f32[1]{0:T(128)S(6)} %copy.9.upper, f32[1]{0:T(128)S(6)} %copy.10.lowest, f32[512,512]{1,0:T(8,128)} %h_hbm.1, f32[512,512]{1,0:T(8,128)} %v_hbm.1), custom_call_target="tpu_custom_call" | custom-call | flops 2415919104 | bytes 3145728 | tf_op jit(solution)/shard_map/pallas_call | solution.py:327
  55.6 2.3 %copy.11 = f32[512,512]{1,0:T(8,128)} copy(f32[512,512]{1,0:T(8,128)} %shard_map.64) | data formatting | bytes 2097152
